TPU v7x, 256 devices: a whole 4x4x8 slice. The times are simulated.
256 devices in a mesh: prow: 8 (over y, core), pcol: 32 (over z, x).
Axes of the slice: x: 4, y: 4, z: 8, core: 2. Of those that a mesh axis runs over, the one named last changes fastest.
Arguments:
- matrix: float32 [8192, 32768], P('prow', 'pcol'), may hold values from -6 to 6
- pivot_inv: float32 [8, 128, 128], replicated, may hold values from -0.06 to 0.16, as said below
- pattern: int32 [64, 256], P('prow', 'pcol'), may hold values 0 or 1
Outputs:
- factored: float32 [8192, 32768], P('prow', 'pcol')
Inputs may be any that keep to these rules, and one draw needn't show every extreme that they name: `pivot_inv`: each block is a positive diagonal plus off-diagonal entries.
All inputs are finite; a program needn't handle non-finite values. No bound on the sum of `pattern` on one device may be relied on, other than what follows from the above.
Results may differ from a plain program's by a relative error of at most 0.0001.
Values sent between devices are 32-bit elements; how exact they have to be, the bound alone decides.
A program may use at most 128 MiB of HBM per device.

v0:
```python
import jax
import jax.numpy as jnp
from jax import lax
from jax.sharding import PartitionSpec as P

BLK = 128
PB = 4
W = 512
STEPS = 2


def from_root(value, axis, source):
    kept = jnp.where(lax.axis_index(axis) == source, value, 0).astype(value.dtype)
    return lax.psum(kept, axis)


def apply_blocks(column, blocks):
    row_count = column.shape[0]
    shaped = column.reshape(row_count, PB, BLK)
    return jnp.einsum("rpk,pkj->rpj", shaped, blocks, precision=lax.Precision.HIGHEST).reshape(
        row_count, W
    )


def shards(matrix, pivot_inv, pattern):
    row_count, col_count = matrix.shape
    keep = jnp.repeat(jnp.repeat(pattern.astype(jnp.float32), BLK, axis=0), BLK, axis=1)
    work = matrix * keep
    row_index = lax.axis_index("prow")
    col_index = lax.axis_index("pcol")
    global_rows = row_index * row_count + jnp.arange(row_count, dtype=jnp.int32)
    global_cols = col_index * col_count + jnp.arange(col_count, dtype=jnp.int32)
    for step_index in range(STEPS):
        first_col = step_index * W
        past_col = first_col + W
        blocks = pivot_inv[step_index * PB : (step_index + 1) * PB]
        below = (global_rows >= past_col)[:, None]
        column = jnp.where(below, work[:, first_col:past_col], 0.0)
        right_side = (global_cols >= past_col)[None, :]
        upper = jnp.where(right_side, work[first_col:past_col, :], 0.0)
        upper_recv = from_root(upper, "prow", 0)
        lower = lax.cond(
            col_index == 0, lambda: apply_blocks(column, blocks), lambda: jnp.zeros_like(column)
        )
        lower_recv = from_root(lower, "pcol", 0)
        update = jnp.dot(
            lower_recv,
            upper_recv,
            precision=lax.Precision.HIGHEST,
            preferred_element_type=jnp.float32,
        )
        work = work - update * keep
        owner_rows = jnp.logical_and(below, col_index == 0)
        work = work.at[:, first_col:past_col].set(
            jnp.where(owner_rows, lower_recv, work[:, first_col:past_col])
        )
    return work


def solution(mesh):
    return jax.shard_map(
        shards,
        mesh=mesh,
        in_specs=(P("prow", "pcol"), P(), P("prow", "pcol")),
        out_specs=P("prow", "pcol"),
        check_vma=False,
    )
```

profile of v0, /device:TPU:40, one launch (start us, length us, event | category | flops | bytes accessed | tf_op | source)
XLA Modules:
  0.0 512.7 jit_solution(10174658490193581103)
XLA Ops:
  6.5 0.7 convert_element_type.13
  7.3 0.0 copy-start.2
  7.3 1.1 broadcast_in_dim.74
  8.4 1.9 copy-done
  10.4 3.5 bitcast_multiply_fusion.2
  13.9 3.4 fusion.13
  17.3 0.0 all-reduce.7.cloned.1.call-update
  17.3 0.0 all-reduce.5.cloned.1.call-start
  17.4 0.2 broadcast_in_dim.75
  17.6 0.7 copy-done.5
  18.3 1.6 conditional.2
  18.3 1.6 broadcast.98.clone
  19.9 1.5 broadcast_select_fusion.1
  21.5 0.0 all-reduce.5.cloned.1.call-update
  21.5 0.0 all-reduce.11.cloned.1.call-start
  21.6 0.7 compare_reduce_fusion.2
  22.2 66.2 %all-reduce.7.cloned.1.call-done = f32[512,1024]{1,0:T(8,128)} async-done(((f32[512,1024]{1,0:T(8,128)}), f32[512,1024]{1,0:T(8,128)}) %all-reduce.7.cloned.1.call-update) | async-done | bytes 2097168 | tf_op jit(solution)/shard_map/psum | solution.py:14
  88.4 158.3 %all-reduce.5.cloned.1.call-done = f32[1024,512]{1,0:T(8,128)} async-done(((f32[1024,512]{1,0:T(8,128)}), f32[1024,512]{1,0:T(8,128)}) %all-reduce.5.cloned.1.call-update) | async-done | bytes 2097168 | tf_op jit(solution)/shard_map/psum | solution.py:14
  246.7 12.5 %fusion.8 = f32[1024,1024]{1,0:T(8,128)S(1)} fusion(f32[128,8,8,128]{3,2,1,0:T(8,128)} %bitcast.37, f32[1024,512]{1,0:T(8,128)} %all-reduce.5.cloned.1.call-done, f32[512,1024]{1,0:T(8,128)} %all-reduce.7.cloned.1.call-done, f32[1024,1024]{1,0:T(8,128)} %param.11), kind=kOutput, calls=%fused_computation.15 | convolution fusion | flops 6445596672 | bytes 16777216 | tf_op jit(solution)/shard_map/dot_general | solution.py:46
  259.3 1.0 fusion.10
  260.3 2.0 copy-done.1
  262.3 1.6 fusion.12
  263.9 0.0 all-reduce.11.cloned.1.call-update
  263.9 0.0 all-reduce.9.cloned.1.call-start
  264.0 1.7 conditional.3
  264.0 1.6 broadcast.100.clone
  265.6 1.5 broadcast_select_fusion
  267.1 0.0 all-reduce.9.cloned.1.call-update
  267.2 63.8 %all-reduce.11.cloned.1.call-done = f32[512,1024]{1,0:T(8,128)} async-done(((f32[512,1024]{1,0:T(8,128)}), f32[512,1024]{1,0:T(8,128)}) %all-reduce.11.cloned.1.call-update) | async-done | bytes 2097168 | tf_op jit(solution)/shard_map/psum | solution.py:14
  331.0 158.6 %all-reduce.9.cloned.1.call-done = f32[1024,512]{1,0:T(8,128)} async-done(((f32[1024,512]{1,0:T(8,128)}), f32[1024,512]{1,0:T(8,128)}) %all-reduce.9.cloned.1.call-update) | async-done | bytes 2097168 | tf_op jit(solution)/shard_map/psum | solution.py:14
  489.6 13.4 %fusion.9 = f32[1024,1024]{1,0:T(8,128)} fusion(f32[1024,1024]{1,0:T(8,128)} %copy-done.1, f32[128,8,8,128]{3,2,1,0:T(8,128)} %bitcast.38, f32[1024,512]{1,0:T(8,128)} %all-reduce.9.cloned.1.call-done, f32[512,1024]{1,0:T(8,128)} %all-reduce.11.cloned.1.call-done), kind=kOutput, calls=%fused_computation.16 | convolution fusion | flops 6444548096 | bytes 16777216 | tf_op jit(solution)/shard_map/dot_general | solution.py:46
  503.0 3.2 fusion.11
  (15 shorter events, 0.1 us)
Async XLA Ops:
  6.5 81.9 %all-reduce.7.cloned.1.call-start = ((), (), s32[]{:S(2)}) async-start(), calls=%async_computation.1 | async-start | bytes 4194304 | tf_op jit(solution)/shard_map/psum | solution.py:14
  7.3 3.1 copy-start.2
  8.4 1.9 copy-start
  17.3 1.0 copy-start.5
  17.3 229.4 %all-reduce.5.cloned.1.call-start = ((), (), s32[]{:S(2)}) async-start(), calls=%async_computation | async-start | bytes 4194304 | tf_op jit(solution)/shard_map/psum | solution.py:14
  21.5 309.5 %all-reduce.11.cloned.1.call-start = ((), (), s32[]{:S(2)}) async-start(), calls=%async_computation.3 | async-start | bytes 4194304 | tf_op jit(solution)/shard_map/psum | solution.py:14
  246.7 12.5 %copy-start.3 = (f32[1024,512]{1,0:T(8,128)S(1)}, f32[1024,512]{1,0:T(8,128)}, u32[]{:S(2)}) copy-start(f32[1024,512]{1,0:T(8,128)} %all-reduce.5.cloned.1.call-done) | copy-start | bytes 6291460
  260.3 2.0 copy-start.1
  263.9 225.7 %all-reduce.9.cloned.1.call-start = ((), (), s32[]{:S(2)}) async-start(), calls=%async_computation.2 | async-start | bytes 4194304 | tf_op jit(solution)/shard_map/psum | solution.py:14
  489.6 13.4 %copy-start.4 = (f32[1024,512]{1,0:T(8,128)S(1)}, f32[1024,512]{1,0:T(8,128)}, u32[]{:S(2)}) copy-start(f32[1024,512]{1,0:T(8,128)} %all-reduce.9.cloned.1.call-done) | copy-start | bytes 6291460
Sparse Core Ops, SparseCore 0:
  17.4 70.9 all-reduce.6
  91.9 154.7 all-reduce.4
  264.0 66.9 all-reduce.10
  334.8 154.7 all-reduce.8
where the time goes:
time: 515 us; the launch traced here: 513 us
  waiting for transfers between devices  447 us (87%)
  matrix products  25.9 us (5%)
  other arithmetic  17.2 us (3%)
  between operations  13.2 us (3%)
  local copies, waits for them, and re-layouts  9.33 us (2%)
    psum x4, waiting for transfers between devices, from_root(): return lax.psum(kept, axis)  447 us
    dot_general x2, matrix products, shards(): jnp.dot(lower_recv, upper_recv, precision=lax.Precision.HIGHEST, preferre...  25.9 us
  transfers between devices with their start and end apart: 4, of which 4 were waited for; matrix products, arithmetic and copies ran while one was open for 1% of the time, Pallas kernels for 0%

commit v1 on v0

v1 whole, which is shorter than its diff:
```python
import functools

import jax
import jax.numpy as jnp
from jax import lax
from jax.experimental import pallas as pl
from jax.experimental.pallas import tpu as pltpu
from jax.sharding import PartitionSpec as P

MESH = pl.DeviceIdType.MESH
B = 128
NX, NY, NZ = 4, 4, 8
TICKS = 16
LAG0 = 13
LAG1 = 18

CHILD = (
    (105276967, 572662304, 201327138, 639633410),
    (1073746192, 1073844624, 29323537, 1073758436),
)
DEPTH = (
    (1515870810, 2995618556, 3456105856),
    (1515870810, 3219398634, 4294960132),
)
ROOT_WAY = (0, 2, 1, 3)


def bit(mask, n):
    low, high = mask & 0xFFFF, mask >> 16
    half = jnp.where(n >= 16, jnp.int32(high), jnp.int32(low))
    return lax.rem(lax.shift_right_logical(half, lax.rem(n, 16)), 2)


def split(value):
    high = value.astype(jnp.bfloat16)
    return high, (value - high.astype(jnp.float32)).astype(jnp.bfloat16)


def dot3(a, b):
    (ah, al), (bh, bl) = a, b
    mul = functools.partial(jnp.dot, preferred_element_type=jnp.float32)
    return mul(ah, bl) + mul(al, bh) + mul(ah, bh)


def at(index, size=B):
    return pl.ds(pl.multiple_of(index * size, size), size)


def kernel(
    a_hbm, pinv, pat, out,
    a, lbuf, ubuf, lhi, llo, uhi, ulo,
    lrecv, urecv, lsend, hsend, usend, uhand, load_sem, out_sem,
):
    p, q = lax.axis_index("prow"), lax.axis_index("pcol")
    y, core = lax.div(p, 2), lax.rem(p, 2)
    z, x = lax.div(q, NX), lax.rem(q, NX)

    load = pltpu.make_async_copy(a_hbm, a, load_sem)
    load.start()

    xp, xm = lax.rem(x + 1, NX), lax.rem(x + NX - 1, NX)
    zp, zm = lax.rem(z + 1, NZ), lax.rem(z + NZ - 1, NZ)
    yp, ym = lax.rem(y + 1, NY), lax.rem(y + NY - 1, NY)
    ways = (z * NX + xp, z * NX + xm, zp * NX + x, zm * NX + x)
    rows = (yp * 2 + core, ym * 2 + core)
    mate = y * 2 + 1 - core

    barrier = pltpu.get_barrier_semaphore()
    greet = [{"prow": mate, "pcol": q}] + [{"prow": r, "pcol": q} for r in rows]
    for w in ways:
        greet += [{"prow": p, "pcol": w}, {"prow": mate, "pcol": w}]
    for device in greet:
        pl.semaphore_signal(barrier, inc=1, device_id=device, device_id_type=MESH)
    pl.semaphore_wait(barrier, len(greet))
    load.wait()

    def send_l(stream, slot, way, first=1, count=None):
        part = slot if count is None else pl.ds(slot, count)
        return pltpu.make_async_remote_copy(
            src_ref=lbuf.at[stream, part],
            dst_ref=lbuf.at[stream, part],
            send_sem=lsend.at[stream, way],
            recv_sem=lrecv.at[stream, slot],
            device_id={"prow": y * 2 + 1, "pcol": ways[way]},
            device_id_type=MESH,
        )

    def hand_l(slot, count=None):
        part = slot if count is None else pl.ds(slot, count)
        return pltpu.make_async_remote_copy(
            src_ref=lbuf.at[0, part],
            dst_ref=lbuf.at[0, part],
            send_sem=hsend,
            recv_sem=lrecv.at[0, slot],
            device_id={"prow": mate, "pcol": q},
            device_id_type=MESH,
        )

    def send_u(slot, way, count=None):
        part = slot if count is None else pl.ds(slot, count)
        return pltpu.make_async_remote_copy(
            src_ref=ubuf.at[part],
            dst_ref=ubuf.at[part],
            send_sem=usend.at[way],
            recv_sem=urecv.at[slot],
            device_id={"prow": rows[way], "pcol": q},
            device_id_type=MESH,
        )

    def hand_u(slot, count=None):
        part = slot if count is None else pl.ds(slot, count)
        return pltpu.make_async_remote_copy(
            src_ref=ubuf.at[part],
            dst_ref=ubuf.at[part],
            send_sem=uhand,
            recv_sem=urecv.at[slot],
            device_id={"prow": mate, "pcol": q},
            device_id_type=MESH,
        )

    def wait_l(stream, slot):
        send_l(stream, slot, 0).wait_recv()

    def wait_u(slot):
        send_u(slot, 0).wait_recv()

    def slot_l(i, t, stream):
        if stream == 1:
            return 4 * i + t
        return jnp.where(y == 0, t * 8 + 4 + i, 4 * i + t)

    def slot_u(tick, way, h):
        j = 2 * tick + h
        return jnp.where(
            q == 0, (2 * way + h) * 8 + 4 + tick, lax.div(j, 4) * 8 + 4 * way + lax.rem(j, 4)
        )

    def mask_all():
        def body(n, _):
            i, j = lax.div(n, 8), lax.rem(n, 8)
            a[at(i), at(j)] = a[at(i), at(j)] * pat[i, j].astype(jnp.float32)
            return 0

        lax.fori_loop(0, 64, body, 0)

    def write_out():
        copy = pltpu.make_async_copy(a, out, out_sem)
        copy.start()
        copy.wait()

    def relay_u(tick, way):
        for h in (0, 1):
            slot = slot_u(tick, way, h)
            wait_u(slot)
            on = y < NY - 1 if way == 0 else y > 1
            pl.when(on)(lambda: send_u(slot, way).start())
            hand_u(slot).start()

    def relay_u_step(k, ticks):
        for way in (0, 1):
            tick = k - 3 * (y if way == 0 else NY - y)
            pl.when((tick >= 0) & (tick < ticks))(lambda: relay_u(tick, way))

    def end_relay_u(ticks):
        pl.when(y < NY - 1)(lambda: send_u(0, 0, 2 * ticks).wait_send())
        pl.when(y > 1)(lambda: send_u(0, 1, 2 * ticks).wait_send())
        hand_u(0, 4 * ticks).wait_send()

    def split_l(stream, pair):
        def body(i, _):
            for h in (0, 1):
                hi, lo = split(lbuf[stream, (2 * pair + h) * 8 + i])
                lhi[at(i), h * B : (h + 1) * B] = hi
                llo[at(i), h * B : (h + 1) * B] = lo
            return 0

        lax.fori_loop(0, 8, body, 0)

    def split_u(pair):
        def body(j, _):
            for h in (0, 1):
                hi, lo = split(ubuf[(2 * pair + h) * 8 + j])
                uhi[h * B : (h + 1) * B, at(j)] = hi
                ulo[h * B : (h + 1) * B, at(j)] = lo
            return 0

        lax.fori_loop(0, 8, body, 0)

    def out_tile(tile):
        return pltpu.make_async_copy(a.at[:, at(tile, 256)], out.at[:, at(tile, 256)], out_sem)

    def piece(n, stream):
        pair, tile = lax.div(n, 4), lax.rem(n, 4)

        @pl.when(tile == 0)
        def _():
            def body(i, _):
                if stream == 0:
                    wait_l(0, pair * 16 + i)
                else:
                    wait_u(pair * 16 + i)
                return 0

            lax.fori_loop(0, 16, body, 0)
            split_l(stream, pair)
            split_u(pair)

        cols = at(tile, 256)
        right = (uhi[0:256, cols], ulo[0:256, cols])

        def rows_body(r, _):
            part = at(r, 256)
            a[part, cols] -= dot3((lhi[part, 0:256], llo[part, 0:256]), right)
            return 0

        lax.fori_loop(0, 4, rows_body, 0)

        @pl.when(pair == 3)
        def _():
            def body(i, _):
                for h in (0, 1):
                    c = at(2 * tile + h)
                    a[at(i), c] = a[at(i), c] * pat[i, 2 * tile + h].astype(jnp.float32)
                return 0

            lax.fori_loop(0, 8, body, 0)
            out_tile(tile).start()

    def end_tiles():
        pltpu.make_async_copy(a, out, out_sem).wait()

    def general0():
        def body(k, _):
            relay_u_step(k, TICKS)
            n = k - LAG0
            pl.when(n >= 0)(lambda: piece(n, 0))
            return 0

        lax.fori_loop(0, LAG0 + 16, body, 0)
        end_relay_u(TICKS)
        end_tiles()

    def general1():
        node = q
        mirror = lax.rem(NZ - z, NZ) * NX + lax.rem(NX - x, NX)
        sends, depths = [], []
        for t in range(4):
            n = node if t < 2 else mirror
            tree = t % 2
            flip = 0 if t < 2 else 1
            sends.append([bit(CHILD[tree][w ^ flip], n) for w in range(4)])
            depths.append(sum(bit(DEPTH[tree][b], n) * (1 << b) for b in range(3)))

        def relay(i, t):
            def one(stream):
                slot = slot_l(i, t, stream)
                wait_l(stream, slot)
                for w in range(4):
                    pl.when(sends[t][w] == 1)(lambda: send_l(stream, slot, w).start())
                if stream == 0:
                    hand_l(slot).start()

            pl.when((y > 0) | (i < 4))(lambda: one(0))
            one(1)

        def body(k, _):
            for t in range(4):
                i = k - 2 * depths[t]
                pl.when((i >= 0) & (i < TICKS))(lambda: relay(i, t))
            n = k - LAG1
            pl.when(n >= 0)(lambda: piece(n, 1))
            return 0

        lax.fori_loop(0, LAG1 + 16, body, 0)
        for w in range(4):
            any_way = sum(sends[t][w] for t in range(4))

            @pl.when(any_way > 0)
            def _():
                send_l(1, 0, w, count=TICKS).wait_send()
                pl.when(y > 0)(lambda: send_l(0, 0, w, count=TICKS).wait_send())
                pl.when(y == 0)(lambda: send_l(0, 0, w, count=4).wait_send())

        pl.when(y > 0)(lambda: hand_l(0, count=64).wait_send())
        pl.when(y == 0)(lambda: hand_l(0, count=16).wait_send())
        end_tiles()

    def upper_root():
        mask_all()
        for kb in range(4):
            def body(j, _):
                ubuf[kb * 8 + j] = a[kb * B : (kb + 1) * B, at(j)]
                return 0

            lax.fori_loop(0, 8, body, 0)
            for j in range(4):
                for way in (0, 1):
                    slot = kb * 8 + 4 * way + j
                    send_u(slot, way).start()
                    hand_u(slot).start()
        def body(j, _):
            for kb in range(4):
                hi, lo = split(a[kb * B : (kb + 1) * B, at(j)])
                uhi[kb * B : (kb + 1) * B, at(j)] = hi
                ulo[kb * B : (kb + 1) * B, at(j)] = lo
            return 0

        lax.fori_loop(0, 8, body, 0)

        def step(i, _):
            for t in range(4):
                wait_l(0, t * 8 + 4 + i)
                hi, lo = split(lbuf[0, t * 8 + 4 + i])
                lhi[0:B, t * B : (t + 1) * B] = hi
                llo[0:B, t * B : (t + 1) * B] = lo
            r = at(4 + i)

            def tile_body(tile, _):
                c = at(tile, 256)
                prod = dot3((lhi[0:B, :], llo[0:B, :]), (uhi[:, c], ulo[:, c]))
                for h in (0, 1):
                    j = 2 * tile + h
                    keep = pat[4 + i, j].astype(jnp.float32)
                    block = a[r, at(j)] - prod[:, h * B : (h + 1) * B] * keep
                    a[r, at(j)] = block
                    ubuf[(4 + i) * 8 + j] = block
                return 0

            lax.fori_loop(0, 4, tile_body, 0)
            for j in range(4):
                for way in (0, 1):
                    slot = (4 + i) * 8 + 4 * way + j
                    send_u(slot, way).start()
                    hand_u(slot).start()
            return 0

        lax.fori_loop(0, 4, step, 0)
        write_out()
        for way in (0, 1):
            send_u(0, way, 32).wait_send()
        hand_u(0, 64).wait_send()

    def corner():
        mask_all()
        for kb in range(4):
            for j in range(4):
                ubuf[kb * 8 + 4 + j] = a[kb * B : (kb + 1) * B, (4 + j) * B : (5 + j) * B]
        for tick in range(4):
            for h in (0, 1):
                for way in (0, 1):
                    slot = (2 * way + h) * 8 + 4 + tick
                    send_u(slot, way).start()
                    hand_u(slot).start()
        for kb in range(4):
            c = slice(kb * B, (kb + 1) * B)
            low = dot3(split(a[512:1024, c]), split(pinv[kb]))
            a[512:1024, c] = low
            lhi[512:1024, c], llo[512:1024, c] = split(low)
            for i in range(4):
                lbuf[0, kb * 8 + 4 + i] = low[i * B : (i + 1) * B]
        for i in range(4):
            for t in range(4):
                send_l(0, t * 8 + 4 + i, ROOT_WAY[t]).start()
        for j in range(4):
            c = slice((4 + j) * B, (5 + j) * B)
            prod = dot3((lhi[512:1024, :], llo[512:1024, :]), split(a[0:512, c]))
            for i in range(4):
                r = slice((4 + i) * B, (5 + i) * B)
                keep = pat[4 + i, 4 + j].astype(jnp.float32)
                a[r, c] = a[r, c] - prod[i * B : (i + 1) * B] * keep
        write_out()
        for way in (0, 1):
            send_u(0, way, 8).wait_send()
        hand_u(0, 16).wait_send()
        for t in range(4):
            send_l(0, 0, t, count=4).wait_send()

    def lower_root(stream):
        mask_all()

        def send_block_column(kb):
            for i in range(2):
                for t in range(4):
                    slot = kb * 8 + 4 * i + t
                    send_l(stream, slot, ROOT_WAY[t]).start()

        def first(kb, _):
            c = at(kb)
            right = split(pinv[kb])

            def rows_body(r, _):
                part = at(r, 256)
                low = dot3(split(a[part, c]), right)
                a[part, c] = low
                lhi[part, c], llo[part, c] = split(low)
                for h in (0, 1):
                    lbuf[stream, kb * 8 + 2 * r + h] = low[h * B : (h + 1) * B]
                return 0

            lax.fori_loop(0, 4, rows_body, 0)
            send_block_column(kb)
            return 0

        lax.fori_loop(0, 4, first, 0)

        def second(j):
            c = at(4 + j)
            if stream == 1:
                for kb in range(4):
                    wait_u(kb * 8 + 4 + j)
            for kb in range(4):
                hi, lo = split(ubuf[kb * 8 + 4 + j])
                uhi[kb * B : (kb + 1) * B, 0:B] = hi
                ulo[kb * B : (kb + 1) * B, 0:B] = lo
            inverse = split(pinv[4 + j])

            def rows_body(r, _):
                part = at(r, 256)
                prod = dot3((lhi[part, :], llo[part, :]), (uhi[:, 0:B], ulo[:, 0:B]))
                for h in (0, 1):
                    rb = 2 * r + h
                    keep = pat[rb, 4 + j].astype(jnp.float32)
                    a[at(rb), c] = a[at(rb), c] - prod[h * B : (h + 1) * B] * keep
                low = dot3(split(a[part, c]), inverse)
                a[part, c] = low
                for h in (0, 1):
                    lbuf[stream, (4 + j) * 8 + 2 * r + h] = low[h * B : (h + 1) * B]
                return 0

            lax.fori_loop(0, 4, rows_body, 0)
            send_block_column(4 + j)

        if stream == 0:
            def body(k, _):
                relay_u_step(k, 4)
                pl.when(k >= 10)(lambda: second(k - 10))
                return 0

            lax.fori_loop(0, 14, body, 0)
        else:
            def body(j, _):
                second(j)
                return 0

            lax.fori_loop(0, 4, body, 0)
        write_out()
        if stream == 0:
            end_relay_u(4)
        for t in range(4):
            send_l(stream, 0, t, count=TICKS).wait_send()

    pl.when((q == 0) & (p == 0))(corner)
    pl.when((q == 0) & (core == 0) & (p > 0))(lambda: lower_root(0))
    pl.when((q == 0) & (core == 1))(lambda: lower_root(1))
    pl.when((q > 0) & (p == 0))(upper_root)
    pl.when((q > 0) & (core == 0) & (p > 0))(general0)
    pl.when((q > 0) & (core == 1))(general1)


def shards(matrix, pivot_inv, pattern):
    f32, bf16 = jnp.float32, jnp.bfloat16
    return pl.pallas_call(
        kernel,
        out_shape=jax.ShapeDtypeStruct(matrix.shape, f32),
        in_specs=[
            pl.BlockSpec(memory_space=pl.ANY),
            pl.BlockSpec(memory_space=pltpu.VMEM),
            pl.BlockSpec(memory_space=pltpu.SMEM),
        ],
        out_specs=pl.BlockSpec(memory_space=pl.ANY),
        scratch_shapes=[
            pltpu.VMEM((1024, 1024), f32),
            pltpu.VMEM((2, 64, B, B), f32),
            pltpu.VMEM((64, B, B), f32),
            pltpu.VMEM((1024, 512), bf16),
            pltpu.VMEM((1024, 512), bf16),
            pltpu.VMEM((512, 1024), bf16),
            pltpu.VMEM((512, 1024), bf16),
            pltpu.SemaphoreType.DMA((2, 64)),
            pltpu.SemaphoreType.DMA((64,)),
            pltpu.SemaphoreType.DMA((2, 4)),
            pltpu.SemaphoreType.DMA,
            pltpu.SemaphoreType.DMA((2,)),
            pltpu.SemaphoreType.DMA,
            pltpu.SemaphoreType.DMA,
            pltpu.SemaphoreType.DMA,
        ],
        compiler_params=pltpu.CompilerParams(
            collective_id=0, has_side_effects=True, vmem_limit_bytes=48 << 20
        ),
        cost_estimate=pl.CostEstimate(
            flops=6 * 1024**3, bytes_accessed=8 << 20, transcendentals=0
        ),
        name="factor",
    )(matrix, pivot_inv, pattern)


def solution(mesh):
    return jax.shard_map(
        shards,
        mesh=mesh,
        in_specs=(P("prow", "pcol"), P(), P("prow", "pcol")),
        out_specs=P("prow", "pcol"),
        check_vma=False,
    )
```

time: 515 us -> 71.5 us (0.14)
  waiting for transfers between devices: 447 us -> 0 us
  Pallas kernels: 0 us -> 66.4 us
  matrix products: 25.9 us -> 0 us
  other arithmetic: 17.2 us -> 0 us
  between operations: 13.2 us -> 0.01 us
  local copies, waits for them, and re-layouts: 9.33 us -> 3.74 us
    psum x4 -> x0, waiting for transfers between devices: 447 us -> none  [from_root(): return lax.psum(kept, axis)]
    pallas_call x0 -> x1, Pallas kernels: none -> 66.4 us  [shards(): pl.pallas_call(kernel, out_shape=jax.ShapeDtypeStruct(matrix.shape, f32),...]
    dot_general x2 -> x0, matrix products: 25.9 us -> none  [shards(): jnp.dot(lower_recv, upper_recv, precision=lax.Precision.HIGHEST, preferre...]
    select_n x4 -> x0, other arithmetic: 8.02 us -> none  [from_root(): jnp.where(lax.axis_index(axis) == source, value, 0).astype(value.dtype)]
  transfers between devices with their start and end apart: 4 -> 0, of which waited for: 4 -> 0; matrix products, arithmetic and copies ran while one was open for 1% -> 0% of each run, Pallas kernels for 0% -> 0%
where the time goes in v1:
time: 71.5 us; the launch traced here: 70.2 us
  Pallas kernels  66.4 us (93%)
  local copies, waits for them, and re-layouts  3.74 us (5%)
    pallas_call x1, Pallas kernels, shards(): pl.pallas_call(kernel, out_shape=jax.ShapeDtypeStruct(matrix.shape, f32),...  66.4 us
    unnamed x5, local copies, waits for them, and re-layouts  3.74 us

profile of v1, /device:TPU:40, one launch (start us, length us, event | category | flops | bytes accessed | tf_op | source)
XLA Modules:
  0.0 70.2 jit_solution(11993350087698417995)
XLA Ops:
  0.0 0.0 copy-start
  0.0 1.0 %copy-done = f32[8,128,128]{2,1,0:T(8,128)S(1)} copy-done((f32[8,128,128]{2,1,0:T(8,128)S(1)}, f32[8,128,128]{2,1,0:T(8,128)}, u32[]{:S(2)}) %copy-start) | copy-done | bytes 524312
  1.0 0.0 copy-start.1
  1.0 0.7 copy-done.1
  1.7 66.4 %factor.1 = f32[1024,1024]{1,0:T(8,128)S(1)} custom-call(f32[1024,1024]{1,0:T(8,128)} %a_hbm.1, f32[8,128,128]{2,1,0:T(8,128)S(1)} %copy-done, s32[8,8]{1,0:T(8,128)S(1)} %copy-done.1), custom_call_target="tpu_custom_call" | custom-call | flops 6442450944 | bytes 8388608 | tf_op jit(solution)/shard_map/factor/pallas_call | solution.py:462
  68.2 2.0 %copy.5 = f32[1024,1024]{1,0:T(8,128)} copy(f32[1024,1024]{1,0:T(8,128)S(1)} %factor.1) | data formatting | bytes 8388608
Async XLA Ops:
  0.0 1.0 %copy-start = (f32[8,128,128]{2,1,0:T(8,128)S(1)}, f32[8,128,128]{2,1,0:T(8,128)}, u32[]{:S(2)}) copy-start(f32[8,128,128]{2,1,0:T(8,128)} %pinv.1) | copy-start | bytes 1572868
  1.0 0.7 copy-start.1

commit v2 on v0

v2 whole, which is shorter than its diff:
```python
import functools

import jax
import jax.numpy as jnp
from jax import lax
from jax.experimental import pallas as pl
from jax.experimental.pallas import tpu as pltpu
from jax.sharding import PartitionSpec as P

MESH = pl.DeviceIdType.MESH
B = 128
NX, NY, NZ = 4, 4, 8
R = 2
TICKS_L = 16 * R
TICKS_U = 16

CHILD = (
    (105276967, 572662304, 201327138, 639633410),
    (1073746192, 1073844624, 29323537, 1073758436),
)
DEPTH = (
    (1515870810, 2995618556, 3456105856),
    (1515870810, 3219398634, 4294960132),
)
ROOT_WAY = (0, 2, 1, 3)


def bit(mask, n):
    low, high = mask & 0xFFFF, mask >> 16
    half = jnp.where(n >= 16, jnp.int32(high), jnp.int32(low))
    return lax.rem(lax.shift_right_logical(half, lax.rem(n, 16)), 2)


def lag(depth):
    return {1: 3, 2: 4, 4: 7}[R] * depth


def split(value):
    high = value.astype(jnp.bfloat16)
    return high, (value - high.astype(jnp.float32)).astype(jnp.bfloat16)


def dot3(a, b):
    (ah, al), (bh, bl) = a, b
    mul = functools.partial(jnp.dot, preferred_element_type=jnp.float32)
    return mul(ah, bl) + mul(al, bh) + mul(ah, bh)


def at(index, size=B):
    return pl.ds(pl.multiple_of(index * size, size), size)


def loop(count, body):
    def step(i, _):
        body(i)
        return 0

    lax.fori_loop(0, count, step, 0)


def kernel(
    a_hbm, pinv_hbm, pat_hbm, a, lhi, llo, uhi, ulo,
    lbuf, ubuf, pinv, pat,
    lrecv, crecv, hrecv, urecv, lsend, csend, hsend, usend, uhand, load_sems,
):
    p, q = lax.axis_index("prow"), lax.axis_index("pcol")
    y, core = lax.div(p, 2), lax.rem(p, 2)
    z, x = lax.div(q, NX), lax.rem(q, NX)
    is_root = (q == 0) | (p == 0)

    load = pltpu.make_async_copy(a_hbm, a, load_sems.at[0])
    load_pat = pltpu.make_async_copy(pat_hbm, pat, load_sems.at[1])
    load_pinv = pltpu.make_async_copy(pinv_hbm, pinv, load_sems.at[2])
    load.start()
    load_pat.start()
    pl.when(is_root)(load_pinv.start)

    xp, xm = lax.rem(x + 1, NX), lax.rem(x + NX - 1, NX)
    zp, zm = lax.rem(z + 1, NZ), lax.rem(z + NZ - 1, NZ)
    yp, ym = lax.rem(y + 1, NY), lax.rem(y + NY - 1, NY)
    ways = (z * NX + xp, z * NX + xm, zp * NX + x, zm * NX + x)
    rows = (yp * 2 + core, ym * 2 + core)
    mate = y * 2 + 1 - core

    barrier = pltpu.get_barrier_semaphore()
    greet = [{"prow": mate, "pcol": q}] + [{"prow": r, "pcol": q} for r in rows]
    for w in ways:
        greet += [{"prow": p, "pcol": w}, {"prow": mate, "pcol": w}]
    for device in greet:
        pl.semaphore_signal(barrier, inc=1, device_id=device, device_id_type=MESH)
    pl.semaphore_wait(barrier, len(greet))
    load.wait()
    load_pat.wait()
    pl.when(is_root)(load_pinv.wait)

    def part(index, count):
        return index if count is None else pl.ds(index, count)

    def copy_l(ref, send_sem, recv_sem, row, pcol):
        return pltpu.make_async_remote_copy(
            src_ref=ref,
            dst_ref=ref,
            send_sem=send_sem,
            recv_sem=recv_sem,
            device_id={"prow": row, "pcol": pcol},
            device_id_type=MESH,
        )

    def send_l(chunk, way, both, count=None):
        chunks = part(chunk, count)
        ref = lbuf.at[chunks] if both else lbuf.at[chunks, 1]
        return copy_l(ref, lsend.at[way], lrecv.at[chunk], y * 2 + 1, ways[way])

    def send_c(chunk, way, count=None):
        ref = lbuf.at[part(chunk, count), 0]
        return copy_l(ref, csend.at[way], crecv.at[chunk], y * 2 + 1, ways[way])

    def hand_l(slot, count=1):
        ref = lbuf.at[pl.ds(slot * R, count * R), 0]
        return copy_l(ref, hsend, hrecv.at[slot], mate, q)

    def send_u(slot, way, count=None):
        return pltpu.make_async_remote_copy(
            src_ref=ubuf.at[part(slot, count)],
            dst_ref=ubuf.at[part(slot, count)],
            send_sem=usend.at[way],
            recv_sem=urecv.at[slot],
            device_id={"prow": rows[way], "pcol": q},
            device_id_type=MESH,
        )

    def hand_u(slot, count=None):
        return pltpu.make_async_remote_copy(
            src_ref=ubuf.at[part(slot, count)],
            dst_ref=ubuf.at[part(slot, count)],
            send_sem=uhand,
            recv_sem=urecv.at[slot],
            device_id={"prow": mate, "pcol": q},
            device_id_type=MESH,
        )

    def wait_u(slot):
        send_u(slot, 0).wait_recv()

    def keep(i, j):
        return pat[i, j].astype(jnp.float32)

    def put_l(stream, slot, block):
        for h in range(R):
            lbuf[slot * R + h, stream] = block[h * (B // R) : (h + 1) * (B // R)]

    def split_block(stream, slot, row, column):
        for h in range(R):
            hi, lo = split(lbuf[slot * R + h, stream])
            into = pl.ds(pl.multiple_of(row * B + h * (B // R), B // R), B // R)
            lhi[into, column * B : (column + 1) * B] = hi
            llo[into, column * B : (column + 1) * B] = lo

    used, tree_of, depth_of = [jnp.int32(0)] * 4, [jnp.int32(0)] * 4, [jnp.int32(0)] * 4
    depths = []
    for t in range(4):
        n = q if t < 2 else lax.rem(NZ - z, NZ) * NX + lax.rem(NX - x, NX)
        tree, flip = t % 2, 0 if t < 2 else 1
        depths.append(sum(bit(DEPTH[tree][b], n) * (1 << b) for b in range(3)))
        for w in range(4):
            has = bit(CHILD[tree][w ^ flip], n)
            used[w] = used[w] + has
            tree_of[w] = tree_of[w] + has * t
            depth_of[w] = depth_of[w] + has * depths[t]
    deepest = jnp.maximum(functools.reduce(jnp.maximum, depths), 5)

    def ready(pair, stream):
        if stream == 0:
            loop(16, lambda i: hand_l(pair * 16 + i).wait_recv())
        else:
            loop(16, lambda i: wait_u(pair * 16 + i))

        def split_both(i):
            for h in (0, 1):
                slot = (2 * pair + h) * 8 + i
                split_block(stream, slot, i, h)
                hi, lo = split(ubuf[slot])
                uhi[h * B : (h + 1) * B, at(i)] = hi
                ulo[h * B : (h + 1) * B, at(i)] = lo

        loop(8, split_both)

    def piece(n, stream):
        pair, tile = lax.div(n, 4), lax.rem(n, 4)
        pl.when(tile == 0)(lambda: ready(pair, stream))

        @pl.when(pair < 3)
        def _():
            cols = at(tile, 256)
            a[:, cols] -= dot3(
                (lhi[:, 0:256], llo[:, 0:256]), (uhi[0:256, cols], ulo[0:256, cols])
            )

    def general0():
        start = 2 * deepest + 3

        def relay(tick, way):
            for h in (0, 1):
                j = 2 * tick + h
                slot = lax.div(j, 4) * 8 + 4 * way + lax.rem(j, 4)
                wait_u(slot)
                on = y < NY - 1 if way == 0 else y > 1
                pl.when(on)(lambda: send_u(slot, way).start())
                hand_u(slot).start()

        def step(k):
            for way in (0, 1):
                tick = k - 3 * (y if way == 0 else NY - y)
                pl.when((tick >= 0) & (tick < TICKS_U))(lambda: relay(tick, way))
            n = k - start
            pl.when(n >= 0)(lambda: piece(n, 0))

        loop(start + 13, step)
        pl.when(y < NY - 1)(lambda: send_u(0, 0, 32).wait_send())
        pl.when(y > 1)(lambda: send_u(0, 1, 32).wait_send())
        hand_u(0, 64).wait_send()

    def general1(both):
        start = lag(deepest) + 4 * R + (0 if both else 4 * R)
        ticks = TICKS_L + (0 if both else 4 * R)

        def chunk_of(i, t):
            return lax.div(i, R) * (4 * R) + t * R + lax.rem(i, R)

        def hand_block(i, t):
            pl.when(lax.rem(i, R) == R - 1)(lambda: hand_l(4 * lax.div(i, R) + t).start())

        def receive(i, t):
            if both:
                send_l(chunk_of(i, t), 0, True).wait_recv()
                hand_block(i, t)
                return

            @pl.when(i < 4 * R)
            def _():
                send_c(chunk_of(i, t), 0).wait_recv()
                hand_block(i, t)

            @pl.when(i >= 4 * R)
            def _():
                send_l(chunk_of(i - 4 * R, t), 0, False).wait_recv()

        def forward(i, way):
            t = tree_of[way]
            if both:
                send_l(chunk_of(i, t), way, True).start()
                return
            pl.when(i < 4 * R)(lambda: send_c(chunk_of(i, t), way).start())
            pl.when(i >= 4 * R)(lambda: send_l(chunk_of(i - 4 * R, t), way, False).start())

        def step(k):
            for t in range(4):
                i = k - lag(depths[t])
                pl.when((i >= 0) & (i < ticks))(lambda: receive(i, t))
            for way in range(4):
                i = k - lag(depth_of[way])
                pl.when((used[way] == 1) & (i >= 0) & (i < ticks))(lambda: forward(i, way))
            n = k - start
            pl.when((n >= 0) & (lax.rem(n, R) == 0))(lambda: piece(lax.div(n, R), 1))

        loop(start + 12 * R + 1, step)
        for way in range(4):

            @pl.when(used[way] == 1)
            def _():
                send_l(0, way, both, TICKS_L).wait_send()
                if not both:
                    send_c(0, way, 4 * R).wait_send()

        hand_l(0, 64 if both else 16).wait_send()

    def mask_block(i, j):
        block = a[at(i), at(j)] * keep(i, j)
        a[at(i), at(j)] = block
        return block

    def upper_root():
        def send_row(kb):
            for j in range(4):
                for way in (0, 1):
                    slot = kb * 8 + 4 * way + j
                    send_u(slot, way).start()
                    hand_u(slot).start()

        def first(kb):
            def body(j):
                ubuf[kb * 8 + j] = mask_block(kb, j)

            loop(8, body)
            send_row(kb)

        loop(4, first)
        for kb in range(4):
            r = slice(kb * B, (kb + 1) * B)
            uhi[r, :], ulo[r, :] = split(dot3(split(pinv[kb]), split(a[r, :])))

        def second(i):
            for t in range(4):
                hand_l(4 * i + t).wait_recv()
                split_block(0, 4 * i + t, 0, t)
            prod = dot3((lhi[0:B, :], llo[0:B, :]), (uhi[...], ulo[...]))
            for j in range(8):
                c = slice(j * B, (j + 1) * B)
                block = (a[at(4 + i), c] - prod[:, c]) * keep(4 + i, j)
                a[at(4 + i), c] = block
                ubuf[(4 + i) * 8 + j] = block
            send_row(4 + i)

        loop(4, second)
        for way in (0, 1):
            send_u(0, way, 32).wait_send()
        hand_u(0, 64).wait_send()

    def corner():
        def start(i):
            for t in range(4):
                put_l(0, 4 * i + t, mask_block(4 + i, t))
            for h in range(R):
                for t in range(4):
                    send_c((4 * i + t) * R + h, ROOT_WAY[t]).start()
            for kb in range(4):
                slot = kb * 8 + 4 + i
                ubuf[slot] = mask_block(kb, 4 + i)
                send_u(slot, 0).start()
                send_u(slot, 1).start()
                hand_u(slot).start()

        loop(4, start)

        def rest(i):
            for j in range(4):
                mask_block(i, j)

        loop(4, rest)
        for kb in range(4):
            c = slice(kb * B, (kb + 1) * B)
            low = dot3(split(a[512:1024, c]), split(pinv[kb]))
            a[512:1024, c] = low
            lhi[512:1024, c], llo[512:1024, c] = split(low)
        for j in range(4):
            c = slice((4 + j) * B, (5 + j) * B)
            prod = dot3((lhi[512:1024, :], llo[512:1024, :]), split(a[0:512, c]))
            for i in range(4):
                r = slice((4 + i) * B, (5 + i) * B)
                a[r, c] = (a[r, c] - prod[i * B : (i + 1) * B]) * keep(4 + i, 4 + j)
        for way in (0, 1):
            send_u(0, way, 16).wait_send()
        hand_u(0, 16).wait_send()
        for way in range(4):
            send_c(0, way, 4 * R).wait_send()

    def lower_root(stream, both):
        def send_column(kb):
            if stream == 0:
                hand_l(kb * 8, 8).start()
                return
            if both:
                hand_l(kb * 8, 8).wait_recv()
            for i in range(2):
                for h in range(R):
                    for t in range(4):
                        chunk = (kb * 8 + 4 * i + t) * R + h
                        send_l(chunk, ROOT_WAY[t], both).start()

        def put_column(kb, low):
            a[:, at(kb)] = low
            for i in range(8):
                put_l(stream, kb * 8 + i, low[i * B : (i + 1) * B])
            send_column(kb)

        def first(kb):
            loop(8, lambda i: mask_block(i, kb))
            low = dot3(split(a[:, at(kb)]), split(pinv[kb]))
            put_column(kb, low)
            for b in range(4):
                c = slice(b * B, (b + 1) * B)

                @pl.when(kb == b)
                def _():
                    lhi[:, c], llo[:, c] = split(a[:, c])

        loop(4, first)

        def second(j):
            for kb in range(4):
                slot = kb * 8 + 4 + j
                wait_u(slot)
                if stream == 0:
                    hand_u(slot).start()
                    pl.when((y == 1) if kb < 2 else (y == 3))(
                        lambda: send_u(slot, 0 if kb < 2 else 1).start()
                    )
            for kb in range(4):
                r = slice(kb * B, (kb + 1) * B)
                uhi[r, 0:B], ulo[r, 0:B] = split(ubuf[kb * 8 + 4 + j])
            c = at(4 + j)
            prod = dot3((lhi[...], llo[...]), (uhi[:, 0:B], ulo[:, 0:B]))
            for i in range(8):
                r = slice(i * B, (i + 1) * B)
                a[r, c] = (a[r, c] - prod[r]) * keep(i, 4 + j)
            put_column(4 + j, dot3(split(a[:, c]), split(pinv[4 + j])))

        loop(4, second)
        if stream == 0:
            hand_u(0, 16).wait_send()
            pl.when(y == 1)(lambda: send_u(0, 0, 8).wait_send())
            pl.when(y == 3)(lambda: send_u(0, 1, 8).wait_send())
            hand_l(0, 64).wait_send()
        else:
            for way in range(4):
                send_l(0, way, both, TICKS_L).wait_send()

    pl.when((q == 0) & (p == 0))(corner)
    pl.when((q == 0) & (core == 0) & (p > 0))(lambda: lower_root(0, True))
    pl.when((q == 0) & (p == 1))(lambda: lower_root(1, False))
    pl.when((q == 0) & (core == 1) & (p > 1))(lambda: lower_root(1, True))
    pl.when((q > 0) & (p == 0))(upper_root)
    pl.when((q > 0) & (core == 0) & (p > 0))(general0)
    pl.when((q > 0) & (p == 1))(lambda: general1(False))
    pl.when((q > 0) & (core == 1) & (p > 1))(lambda: general1(True))


def finish(a, lhi, llo, uhi, ulo, pat_hbm, out, tiles, pat, pat_sem, out_sems):
    general = (lax.axis_index("prow") > 0) & (lax.axis_index("pcol") > 0)

    @pl.when(general)
    def _():
        load = pltpu.make_async_copy(pat_hbm, pat, pat_sem)
        load.start()
        copies = []
        for tile in range(4):
            cols = slice(tile * 256, (tile + 1) * 256)
            right = (uhi[0:256, cols], ulo[0:256, cols])
            tiles[tile] = a[:, cols] - dot3((lhi[:, 0:256], llo[:, 0:256]), right)
            if tile == 0:
                load.wait()
            for i in range(8):
                for h in (0, 1):
                    r, c = slice(i * B, (i + 1) * B), slice(h * B, (h + 1) * B)
                    keep = pat[i, 2 * tile + h].astype(jnp.float32)
                    tiles[tile, r, c] = tiles[tile, r, c] * keep
            copies.append(
                pltpu.make_async_copy(tiles.at[tile], out.at[:, cols], out_sems.at[tile])
            )
            copies[-1].start()
        for copy in copies:
            copy.wait()

    @pl.when(jnp.logical_not(general))
    def _():
        copy = pltpu.make_async_copy(a, out, out_sems.at[0])
        copy.start()
        copy.wait()


def shards(matrix, pivot_inv, pattern):
    f32, bf16 = jnp.float32, jnp.bfloat16
    in_hbm, in_vmem = pl.BlockSpec(memory_space=pltpu.HBM), pl.BlockSpec(memory_space=pltpu.VMEM)
    parts = pl.pallas_call(
        kernel,
        out_shape=[pltpu.VMEM(matrix.shape, f32)]
        + [pltpu.VMEM((1024, 512), bf16)] * 2
        + [pltpu.VMEM((512, 1024), bf16)] * 2,
        in_specs=[in_hbm] * 3,
        out_specs=[in_vmem] * 5,
        scratch_shapes=[
            pltpu.VMEM((64 * R, 2, B // R, B), f32),
            pltpu.VMEM((64, B, B), f32),
            pltpu.VMEM(pivot_inv.shape, f32),
            pltpu.SMEM(pattern.shape, jnp.int32),
            pltpu.SemaphoreType.DMA((64 * R,)),
            pltpu.SemaphoreType.DMA((16 * R,)),
            pltpu.SemaphoreType.DMA((64,)),
            pltpu.SemaphoreType.DMA((64,)),
            pltpu.SemaphoreType.DMA((4,)),
            pltpu.SemaphoreType.DMA((4,)),
            pltpu.SemaphoreType.DMA,
            pltpu.SemaphoreType.DMA((2,)),
            pltpu.SemaphoreType.DMA,
            pltpu.SemaphoreType.DMA((3,)),
        ],
        compiler_params=pltpu.CompilerParams(
            collective_id=0, has_side_effects=True, vmem_limit_bytes=50 << 20
        ),
        cost_estimate=pl.CostEstimate(
            flops=5 * 1024**3, bytes_accessed=8 << 20, transcendentals=0
        ),
        name="factor",
    )(matrix, pivot_inv, pattern)
    return pl.pallas_call(
        finish,
        out_shape=jax.ShapeDtypeStruct(matrix.shape, f32),
        in_specs=[in_vmem] * 5 + [in_hbm],
        out_specs=in_hbm,
        scratch_shapes=[
            pltpu.VMEM((4, 1024, 256), f32),
            pltpu.SMEM(pattern.shape, jnp.int32),
            pltpu.SemaphoreType.DMA,
            pltpu.SemaphoreType.DMA((4,)),
        ],
        compiler_params=pltpu.CompilerParams(vmem_limit_bytes=12 << 20),
        cost_estimate=pl.CostEstimate(
            flops=3 * 512 * 1024**2, bytes_accessed=8 << 20, transcendentals=0
        ),
        name="finish",
    )(*parts, pattern)


def solution(mesh):
    return jax.shard_map(
        shards,
        mesh=mesh,
        in_specs=(P("prow", "pcol"), P(), P("prow", "pcol")),
        out_specs=P("prow", "pcol"),
        check_vma=False,
    )
```

time: 515 us -> 60.5 us (0.12)
  the two profiles are of different devices: /device:TPU:40 before, /device:TPU:56 now
where the time goes in v2:
time: 60.5 us; the launch traced here: 60.4 us
  Pallas kernels  60.2 us (100%)
    pallas_call x1, Pallas kernels, shards(): pl.pallas_call(kernel, out_shape=[pltpu.VMEM(matrix.shape, f32)] + [pltpu...  56.4 us
    pallas_call x1, Pallas kernels, shards(): pl.pallas_call(finish, out_shape=jax.ShapeDtypeStruct(matrix.shape, f32),...  3.8 us

profile of v2, /device:TPU:56, one launch (start us, length us, event | category | flops | bytes accessed | tf_op | source)
XLA Modules:
  0.0 60.4 jit_solution(6755981216014686412)
XLA Ops:
  0.0 0.0 copy-start
  0.0 56.4 %factor.1 = (f32[1024,1024]{1,0:T(8,128)S(1)}, bf16[1024,512]{1,0:T(8,128)(2,1)S(1)}, bf16[1024,512]{1,0:T(8,128)(2,1)S(1)}, bf16[512,1024]{1,0:T(8,128)(2,1)S(1)}, bf16[512,1024]{1,0:T(8,128)(2,1)S(1)}) custom-call(f32[1024,1024]{1,0:T(8,128)} %a_hbm.1, f32[8,128,128]{2,1,0:T(8,128)} %pinv_hbm.1, s32[8,8]{1,0:T(8,128)} %pat_hbm.3), custom_call_target="tpu_custom_call" | custom-call | flops 5368709120 | bytes 8388608 | tf_op jit(solution)/shard_map/factor/pallas_call | solution.py:464
  56.4 0.0 copy-done
  56.4 3.8 %finish.1 = f32[1024,1024]{1,0:T(8,128)} custom-call(f32[1024,1024]{1,0:T(8,128)S(1)} %get-tuple-element.10.a, bf16[1024,512]{1,0:T(8,128)(2,1)S(1)} %get-tuple-element.11.lhi, bf16[1024,512]{1,0:T(8,128)(2,1)S(1)} %get-tuple-element.12.llo, bf16[512,1024]{1,0:T(8,128)(2,1)S(1)} %get-tuple-element.13.uhi, bf16[512,1024]{1,0:T(8,128)(2,1)S(1)} %get-tuple-element.14.ulo, ...), custom_call_target="tpu_custom_call" | custom-call | flops 1610612736 | bytes 8388608 | tf_op jit(solution)/shard_map/finish/pallas_call | solution.py:495
Async XLA Ops:
  0.0 56.4 %copy-start = (s32[8,8]{1,0:T(8,128)S(1)}, s32[8,8]{1,0:T(8,128)}, u32[]{:S(2)}) copy-start(s32[8,8]{1,0:T(8,128)} %pat_hbm.3) | copy-start | bytes 772

commit v3 on v2

v3 whole, which is shorter than its diff:
```python
import functools

import jax
import jax.numpy as jnp
from jax import lax
from jax.experimental import pallas as pl
from jax.experimental.pallas import tpu as pltpu
from jax.sharding import PartitionSpec as P

MESH = pl.DeviceIdType.MESH
B = 128
NX, NY, NZ = 4, 4, 8
R = 2
TICKS_L = 16 * R
LAG_U = 5

CHILD = (
    (105276967, 572662304, 201327138, 639633410),
    (1073746192, 1073844624, 29323537, 1073758436),
)
DEPTH = (
    (1515870810, 2995618556, 3456105856),
    (1515870810, 3219398634, 4294960132),
)
ROOT_WAY = (0, 2, 1, 3)


def bit(mask, n):
    low, high = mask & 0xFFFF, mask >> 16
    half = jnp.where(n >= 16, jnp.int32(high), jnp.int32(low))
    return lax.rem(lax.shift_right_logical(half, lax.rem(n, 16)), 2)


def lag(depth):
    return {2: 4, 4: 8}[R] * depth


def split(value):
    high = value.astype(jnp.bfloat16)
    return high, (value - high.astype(jnp.float32)).astype(jnp.bfloat16)


def dot3(a, b):
    (ah, al), (bh, bl) = a, b
    mul = functools.partial(jnp.dot, preferred_element_type=jnp.float32)
    return mul(ah, bl) + mul(al, bh) + mul(ah, bh)


def at(index, size=B):
    return pl.ds(pl.multiple_of(index * size, size), size)


def loop(count, body):
    def step(i, _):
        body(i)
        return 0

    lax.fori_loop(0, count, step, 0)


def kernel(
    a_hbm, pinv_hbm, pat_hbm, a, lhi, llo, uhi, ulo,
    lbuf, ubuf, pinv, pat,
    lrecv, crecv, hrecv, urecv, lsend, csend, hsend, usend, uhand, load_sems,
):
    p, q = lax.axis_index("prow"), lax.axis_index("pcol")
    y, core = lax.div(p, 2), lax.rem(p, 2)
    z, x = lax.div(q, NX), lax.rem(q, NX)
    is_root = (q == 0) | (p == 0)

    xp, xm = lax.rem(x + 1, NX), lax.rem(x + NX - 1, NX)
    zp, zm = lax.rem(z + 1, NZ), lax.rem(z + NZ - 1, NZ)
    yp, ym = lax.rem(y + 1, NY), lax.rem(y + NY - 1, NY)
    ways = (z * NX + xp, z * NX + xm, zp * NX + x, zm * NX + x)
    rows = (yp * 2 + core, ym * 2 + core)
    mate = y * 2 + 1 - core

    barrier = pltpu.get_barrier_semaphore()
    greet = [{"prow": mate, "pcol": q}] + [{"prow": r, "pcol": q} for r in rows]
    for w in ways:
        greet += [{"prow": p, "pcol": w}, {"prow": mate, "pcol": w}]
    for device in greet:
        pl.semaphore_signal(barrier, inc=1, device_id=device, device_id_type=MESH)

    load_pat = pltpu.make_async_copy(pat_hbm, pat, load_sems.at[8])
    load_pinv = pltpu.make_async_copy(pinv_hbm, pinv, load_sems.at[9])
    loads = [
        pltpu.make_async_copy(a_hbm.at[at(i)], a.at[at(i)], load_sems.at[i]) for i in range(8)
    ]
    load_pat.start()
    pl.when(is_root)(load_pinv.start)
    for load in loads:
        load.start()

    def part(index, count):
        return index if count is None else pl.ds(index, count)

    def copy_l(ref, send_sem, recv_sem, row, pcol):
        return pltpu.make_async_remote_copy(
            src_ref=ref,
            dst_ref=ref,
            send_sem=send_sem,
            recv_sem=recv_sem,
            device_id={"prow": row, "pcol": pcol},
            device_id_type=MESH,
        )

    def send_l(tick, t, way, both, count=None):
        ref = lbuf.at[part(tick, count), t]
        if not both:
            ref = lbuf.at[part(tick, count), t, 1]
        return copy_l(ref, lsend.at[way], lrecv.at[4 * tick + t], y * 2 + 1, ways[way])

    def root_l(stream, tick, t, count=None):
        ref = lbuf.at[part(tick, count), t, stream]
        way = ROOT_WAY[t]
        return copy_l(ref, lsend.at[way], lrecv.at[4 * tick + t], y * 2 + 1, ways[way])

    def send_c(tick, t, way, count=None):
        ref = lbuf.at[part(tick, count), t, 0]
        return copy_l(ref, csend.at[way], crecv.at[4 * tick + t], y * 2 + 1, ways[way])

    def hand_l(tick, t, count=2):
        ref = lbuf.at[pl.ds(tick, count), t, 0]
        return copy_l(ref, hsend, hrecv.at[4 * tick + t], mate, q)

    def hand_ticks(tick, count):
        ref = lbuf.at[pl.ds(tick, count), :, 0]
        return copy_l(ref, hsend, hrecv.at[4 * tick], mate, q)

    def copy_u(ref, send_sem, slot, row):
        return pltpu.make_async_remote_copy(
            src_ref=ref,
            dst_ref=ref,
            send_sem=send_sem,
            recv_sem=urecv.at[slot],
            device_id={"prow": row, "pcol": q},
            device_id_type=MESH,
        )

    def send_u(slot, half, way):
        return copy_u(ubuf.at[slot, half], usend.at[way], 2 * slot + half, rows[way])

    def hand_u(slot, half):
        return copy_u(ubuf.at[slot, half], uhand, 2 * slot + half, mate)

    def end_u(sem, blocks):
        copy_u(ubuf.at[pl.ds(0, blocks)], sem, 0, mate).wait_send()

    def start_u(slot, ways_out):
        for half in (0, 1):
            for way in ways_out:
                send_u(slot, half, way).start()
            hand_u(slot, half).start()

    def wait_u(slot):
        for half in (0, 1):
            hand_u(slot, half).wait_recv()

    def put_u(slot, block):
        ubuf[slot] = block.reshape(2, B // 2, B)

    def get_u(slot):
        return ubuf[slot].reshape(B, B)

    def keep(i, j):
        return pat[i, j].astype(jnp.float32)

    def put_l(stream, block_tick, t, block):
        for h in range(R):
            rows_of = slice(h * (B // R), (h + 1) * (B // R))
            lbuf[block_tick * R + h, t, stream] = block[rows_of]

    def split_block(stream, block_tick, t, row, column):
        for h in range(R):
            hi, lo = split(lbuf[block_tick * R + h, t, stream])
            into = pl.ds(pl.multiple_of(row * B + h * (B // R), B // R), B // R)
            lhi[into, column * B : (column + 1) * B] = hi
            llo[into, column * B : (column + 1) * B] = lo

    used, tree_of, depth_of = [jnp.int32(0)] * 4, [jnp.int32(0)] * 4, [jnp.int32(0)] * 4
    first_of, leaf = [jnp.int32(0)] * 4, [jnp.int32(1)] * 4
    depths = []
    for t in range(4):
        n = q if t < 2 else lax.rem(NZ - z, NZ) * NX + lax.rem(NX - x, NX)
        tree, flip = t % 2, 0 if t < 2 else 1
        depths.append(sum(bit(DEPTH[tree][b], n) * (1 << b) for b in range(3)))
        for w in range(4):
            has = bit(CHILD[tree][w ^ flip], n)
            first_of[w] = jnp.where((has == 1) & (leaf[t] == 1), 1, first_of[w])
            leaf[t] = jnp.where(has == 1, 0, leaf[t])
            used[w] = used[w] + has
            tree_of[w] = tree_of[w] + has * t
            depth_of[w] = depth_of[w] + has * depths[t]
    deepest = jnp.maximum(functools.reduce(jnp.maximum, depths), 5)

    def ready(pair, stream):
        if stream == 0:

            def wait_tick(i):
                for t in range(4):
                    hand_l(pair * 4 * R + 2 * i, t).wait_recv()

            loop(2 * R, wait_tick)
        else:
            loop(16, lambda i: wait_u(pair * 16 + i))

        def split_both(i):
            for h in (0, 1):
                for half in (0, 1):
                    split_block(stream, 4 * pair + 2 * h + half, i, 4 * half + i, h)
                    j = 4 * half + i
                    hi, lo = split(get_u((2 * pair + h) * 8 + j))
                    uhi[h * B : (h + 1) * B, at(j)] = hi
                    ulo[h * B : (h + 1) * B, at(j)] = lo

        loop(4, split_both)

    def piece(n, stream):
        pair = lax.shift_right_logical(n, 2)
        tile = n - 4 * pair
        pl.when(tile == 0)(lambda: ready(pair, stream))

        @pl.when(pair < 3)
        def _():
            cols = at(tile, 256)
            a[:, cols] -= dot3(
                (lhi[:, 0:256], llo[:, 0:256]), (uhi[0:256, cols], ulo[0:256, cols])
            )

    def general0():
        start = 4 * deepest + 6

        def relay(tick, way):
            row = lax.shift_right_logical(tick, 2)
            slot = 4 * row + 4 * way + tick
            for half in (0, 1):
                hand_u(slot, half).wait_recv()
                on = y < NY - 1 if way == 0 else y > 1
                pl.when(on)(lambda: send_u(slot, half, way).start())
                hand_u(slot, half).start()

        def step(kk):
            for odd in (0, 1):
                for way in (0, 1):
                    tick = 2 * kk + odd - LAG_U * (y if way == 0 else NY - y)
                    pl.when((tick >= 0) & (tick < 32))(lambda: relay(tick, way))
            n = 2 * kk - start
            pl.when(n >= 0)(lambda: piece(lax.shift_right_logical(n, 1), 0))

        loop(lax.shift_right_logical(start, 1) + 13, step)
        pl.when(y < NY - 1)(lambda: end_u(usend.at[0], 32))
        pl.when(y > 1)(lambda: end_u(usend.at[1], 32))
        end_u(uhand, 64)

    def general1(both):
        start = lag(deepest) + 4 * R + (0 if both else 4 * R)
        ticks = TICKS_L + (0 if both else 4 * R)

        def receive(i, t, odd):
            def hand():
                if odd:
                    hand_l(i - 1, t).start()

            if both:
                send_l(i, t, 0, True).wait_recv()
                hand()
                return

            @pl.when(i < 4 * R)
            def _():
                send_c(i, t, 0).wait_recv()
                hand()

            pl.when(i >= 4 * R)(lambda: send_l(i - 4 * R, t, 0, False).wait_recv())

        def forward(i, way):
            t = tree_of[way]
            if both:
                send_l(i, t, way, True).start()
                return
            pl.when(i < 4 * R)(lambda: send_c(i, t, way).start())
            pl.when(i >= 4 * R)(lambda: send_l(i - 4 * R, t, way, False).start())

        last = [jnp.where(used[way] == 1, ticks, 0) for way in range(4)]
        last_leaf = [jnp.where(leaf[t] == 1, ticks, 0) for t in range(4)]
        lags = [lag(d) for d in depths]
        lags_out = [lag(d) for d in depth_of]

        def relay(k, odd):
            for way in range(4):
                i = k - lags_out[way]

                @pl.when((i >= 0) & (i < last[way]))
                def _():
                    pl.when(first_of[way] == 1)(lambda: receive(i, tree_of[way], odd))
                    forward(i, way)

            for t in range(4):
                i = k - lags[t]
                pl.when((i >= 0) & (i < last_leaf[t]))(lambda: receive(i, t, odd))

        def step(kk):
            relay(2 * kk, False)
            relay(2 * kk + 1, True)
            n = 2 * kk - start
            if R == 2:
                pl.when(n >= 0)(lambda: piece(lax.shift_right_logical(n, 1), 1))
            else:
                even = (n & 2) == 0
                pl.when((n >= 0) & even)(lambda: piece(lax.shift_right_logical(n, 2), 1))

        loop(lax.shift_right_logical(start + 12 * R, 1) + 1, step)
        for way in range(4):

            @pl.when(used[way] == 1)
            def _():
                send_l(0, 0, way, both, TICKS_L).wait_send()
                if not both:
                    send_c(0, 0, way, 4 * R).wait_send()

        hand_ticks(0, TICKS_L if both else 4 * R).wait_send()

    def mask_block(i, j):
        block = a[at(i), at(j)] * keep(i, j)
        a[at(i), at(j)] = block
        return block

    def send_row(kb):
        for j in range(4):
            for half in (0, 1):
                for way in (0, 1):
                    slot = kb * 8 + 4 * way + j
                    send_u(slot, half, way).start()
                    hand_u(slot, half).start()

    def prepare_upper():
        def body(j):
            for kb in range(4):
                put_u(kb * 8 + j, mask_block(kb, j))

        loop(8, body)

    def upper_root():
        loop(4, send_row)
        for kb in range(4):
            r = slice(kb * B, (kb + 1) * B)
            uhi[r, :], ulo[r, :] = split(dot3(split(pinv[kb]), split(a[r, :])))

        def second(i):
            for t in range(4):
                for h in range(0, R, 2):
                    hand_l(i * R + h, t).wait_recv()
                split_block(0, i, t, 0, t)
            prod = dot3((lhi[0:B, :], llo[0:B, :]), (uhi[...], ulo[...]))
            for j in range(8):
                c = slice(j * B, (j + 1) * B)
                block = (a[at(4 + i), c] - prod[:, c]) * keep(4 + i, j)
                a[at(4 + i), c] = block
                put_u((4 + i) * 8 + j, block)
            send_row(4 + i)

        loop(4, second)
        for way in (0, 1):
            end_u(usend.at[way], 32)
        end_u(uhand, 64)

    def prepare_corner():
        def body(i):
            for t in range(4):
                put_l(0, i, t, mask_block(4 + i, t))
                put_u(t * 8 + 4 + i, mask_block(t, 4 + i))

        loop(4, body)

    def corner():
        def start(i):
            for h in range(R):
                for t in range(4):
                    send_c(i * R + h, t, ROOT_WAY[t]).start()
            for kb in range(4):
                for half in (0, 1):
                    for way in (0, 1):
                        send_u(kb * 8 + 4 + i, half, way).start()

        loop(4, start)
        for way in range(4):
            send_c(0, 0, way, 4 * R).wait_send()

        def hand(i):
            for kb in range(4):
                for half in (0, 1):
                    hand_u(kb * 8 + 4 + i, half).start()

        loop(4, hand)

        def rest(i):
            for j in range(4):
                mask_block(i, j)

        loop(4, rest)
        for kb in range(4):
            c = slice(kb * B, (kb + 1) * B)
            low = dot3(split(a[512:1024, c]), split(pinv[kb]))
            a[512:1024, c] = low
            lhi[512:1024, c], llo[512:1024, c] = split(low)
        for j in range(4):
            c = slice((4 + j) * B, (5 + j) * B)
            prod = dot3((lhi[512:1024, :], llo[512:1024, :]), split(a[0:512, c]))
            for i in range(4):
                r = slice((4 + i) * B, (5 + i) * B)
                a[r, c] = (a[r, c] - prod[i * B : (i + 1) * B]) * keep(4 + i, 4 + j)
        for way in (0, 1):
            end_u(usend.at[way], 16)
        end_u(uhand, 16)

    def put_column(stream, kb, low):
        a[:, at(kb)] = low
        for i in range(8):
            put_l(stream, 2 * kb + i // 4, i % 4, low[i * B : (i + 1) * B])

    def lower_first(stream, kb):
        loop(8, lambda i: mask_block(i, kb))
        put_column(stream, kb, dot3(split(a[:, at(kb)]), split(pinv[kb])))

    def lower_root(stream, both):
        def send_column(kb):
            for i in range(2 * R):
                for t in range(4):
                    root_l(stream, kb * 2 * R + i, t).start()

        if not both:
            for kb in range(4):
                wait_u(kb * 8 + 4)
        send_column(0)

        def first(kb):
            lower_first(stream, kb + 1)
            send_column(kb + 1)

        loop(3, first)
        lhi[...], llo[...] = split(a[:, 0:512])

        def second(j):
            def arrive():
                for kb in range(4):
                    slot = kb * 8 + 4 + j
                    for half in (0, 1):
                        hand_u(slot, half).wait_recv()
                        if stream == 0:
                            pl.when((y == 1) if kb < 2 else (y == 3))(
                                lambda: send_u(slot, half, 0 if kb < 2 else 1).start()
                            )
                            hand_u(slot, half).start()

            if both:
                arrive()
            else:
                pl.when(j > 0)(arrive)
            for kb in range(4):
                r = slice(kb * B, (kb + 1) * B)
                uhi[r, 0:B], ulo[r, 0:B] = split(get_u(kb * 8 + 4 + j))
            c = at(4 + j)
            prod = dot3((lhi[...], llo[...]), (uhi[:, 0:B], ulo[:, 0:B]))
            for i in range(8):
                r = slice(i * B, (i + 1) * B)
                a[r, c] = (a[r, c] - prod[r]) * keep(i, 4 + j)
            put_column(stream, 4 + j, dot3(split(a[:, c]), split(pinv[4 + j])))
            send_column(4 + j)

        loop(4, second)
        if stream == 0:
            end_u(uhand, 16)
            pl.when(y == 1)(lambda: end_u(usend.at[0], 8))
            pl.when(y == 3)(lambda: end_u(usend.at[1], 8))
        for t in range(4):
            root_l(stream, 0, t, TICKS_L).wait_send()

    is_corner, is_upper = (q == 0) & (p == 0), (q > 0) & (p == 0)
    lower0, lower1 = (q == 0) & (core == 0) & (p > 0), (q == 0) & (core == 1)
    for load in loads:
        load.wait()
    load_pat.wait()
    pl.when(is_root)(load_pinv.wait)
    pl.when(is_corner)(prepare_corner)
    pl.when(is_upper)(prepare_upper)
    pl.when(lower0)(lambda: lower_first(0, 0))
    pl.when(lower1)(lambda: lower_first(1, 0))
    pl.semaphore_wait(barrier, len(greet))

    pl.when(is_corner)(corner)
    pl.when(is_upper)(upper_root)
    pl.when(lower0)(lambda: lower_root(0, True))
    pl.when(lower1 & (p == 1))(lambda: lower_root(1, False))
    pl.when(lower1 & (p > 1))(lambda: lower_root(1, True))
    pl.when((q > 0) & (core == 0) & (p > 0))(general0)
    pl.when((q > 0) & (p == 1))(lambda: general1(False))
    pl.when((q > 0) & (core == 1) & (p > 1))(lambda: general1(True))


def finish(a, lhi, llo, uhi, ulo, pat_hbm, out, tiles, pat, pat_sem, out_sems):
    general = (lax.axis_index("prow") > 0) & (lax.axis_index("pcol") > 0)

    @pl.when(general)
    def _():
        load = pltpu.make_async_copy(pat_hbm, pat, pat_sem)
        load.start()
        copies = []
        for tile in range(4):
            cols = slice(tile * 256, (tile + 1) * 256)
            right = (uhi[0:256, cols], ulo[0:256, cols])
            tiles[tile] = a[:, cols] - dot3((lhi[:, 0:256], llo[:, 0:256]), right)
            if tile == 0:
                load.wait()
            for i in range(8):
                for h in (0, 1):
                    r, c = slice(i * B, (i + 1) * B), slice(h * B, (h + 1) * B)
                    keep = pat[i, 2 * tile + h].astype(jnp.float32)
                    tiles[tile, r, c] = tiles[tile, r, c] * keep
            copies.append(
                pltpu.make_async_copy(tiles.at[tile], out.at[:, cols], out_sems.at[tile])
            )
            copies[-1].start()
        for copy in copies:
            copy.wait()

    @pl.when(jnp.logical_not(general))
    def _():
        copy = pltpu.make_async_copy(a, out, out_sems.at[0])
        copy.start()
        copy.wait()


def shards(matrix, pivot_inv, pattern):
    f32, bf16 = jnp.float32, jnp.bfloat16
    in_hbm, in_vmem = pl.BlockSpec(memory_space=pltpu.HBM), pl.BlockSpec(memory_space=pltpu.VMEM)
    parts = pl.pallas_call(
        kernel,
        out_shape=[pltpu.VMEM(matrix.shape, f32)]
        + [pltpu.VMEM((1024, 512), bf16)] * 2
        + [pltpu.VMEM((512, 1024), bf16)] * 2,
        in_specs=[in_hbm] * 3,
        out_specs=[in_vmem] * 5,
        scratch_shapes=[
            pltpu.VMEM((TICKS_L, 4, 2, B // R, B), f32),
            pltpu.VMEM((64, 2, B // 2, B), f32),
            pltpu.VMEM(pivot_inv.shape, f32),
            pltpu.SMEM(pattern.shape, jnp.int32),
            pltpu.SemaphoreType.DMA((64 * R,)),
            pltpu.SemaphoreType.DMA((16 * R,)),
            pltpu.SemaphoreType.DMA((64 * R,)),
            pltpu.SemaphoreType.DMA((128,)),
            pltpu.SemaphoreType.DMA((4,)),
            pltpu.SemaphoreType.DMA((4,)),
            pltpu.SemaphoreType.DMA,
            pltpu.SemaphoreType.DMA((2,)),
            pltpu.SemaphoreType.DMA,
            pltpu.SemaphoreType.DMA((10,)),
        ],
        compiler_params=pltpu.CompilerParams(
            collective_id=0, has_side_effects=True, vmem_limit_bytes=50 << 20
        ),
        cost_estimate=pl.CostEstimate(
            flops=5 * 1024**3, bytes_accessed=8 << 20, transcendentals=0
        ),
        name="factor",
    )(matrix, pivot_inv, pattern)
    return pl.pallas_call(
        finish,
        out_shape=jax.ShapeDtypeStruct(matrix.shape, f32),
        in_specs=[in_vmem] * 5 + [in_hbm],
        out_specs=in_hbm,
        scratch_shapes=[
            pltpu.VMEM((4, 1024, 256), f32),
            pltpu.SMEM(pattern.shape, jnp.int32),
            pltpu.SemaphoreType.DMA,
            pltpu.SemaphoreType.DMA((4,)),
        ],
        compiler_params=pltpu.CompilerParams(vmem_limit_bytes=12 << 20),
        cost_estimate=pl.CostEstimate(
            flops=3 * 512 * 1024**2, bytes_accessed=8 << 20, transcendentals=0
        ),
        name="finish",
    )(*parts, pattern)


def solution(mesh):
    return jax.shard_map(
        shards,
        mesh=mesh,
        in_specs=(P("prow", "pcol"), P(), P("prow", "pcol")),
        out_specs=P("prow", "pcol"),
        check_vma=False,
    )
```

time: 60.5 us -> 58.4 us (0.965)
  the two profiles are of different devices: /device:TPU:56 before, /device:TPU:40 now
where the time goes in v3:
time: 58.4 us; the launch traced here: 58.3 us
  Pallas kernels  58.1 us (99%)
    pallas_call x1, Pallas kernels, shards(): pl.pallas_call(kernel, out_shape=[pltpu.VMEM(matrix.shape, f32)] + [pltpu...  54.3 us
    pallas_call x1, Pallas kernels, shards(): pl.pallas_call(finish, out_shape=jax.ShapeDtypeStruct(matrix.shape, f32),...  3.8 us

profile of v3, /device:TPU:40, one launch (start us, length us, event | category | flops | bytes accessed | tf_op | source)
XLA Modules:
  0.0 58.3 jit_solution(16712090401468141939)
XLA Ops:
  0.0 0.0 copy-start
  0.0 54.3 %factor.1 = (f32[1024,1024]{1,0:T(8,128)S(1)}, bf16[1024,512]{1,0:T(8,128)(2,1)S(1)}, bf16[1024,512]{1,0:T(8,128)(2,1)S(1)}, bf16[512,1024]{1,0:T(8,128)(2,1)S(1)}, bf16[512,1024]{1,0:T(8,128)(2,1)S(1)}) custom-call(f32[1024,1024]{1,0:T(8,128)} %a_hbm.1, f32[8,128,128]{2,1,0:T(8,128)} %pinv_hbm.1, s32[8,8]{1,0:T(8,128)} %pat_hbm.3), custom_call_target="tpu_custom_call" | custom-call | flops 5368709120 | bytes 8388608 | tf_op jit(solution)/shard_map/factor/pallas_call | solution.py:537
  54.3 0.0 copy-done
  54.3 3.8 %finish.1 = f32[1024,1024]{1,0:T(8,128)} custom-call(f32[1024,1024]{1,0:T(8,128)S(1)} %get-tuple-element.10.a, bf16[1024,512]{1,0:T(8,128)(2,1)S(1)} %get-tuple-element.11.lhi, bf16[1024,512]{1,0:T(8,128)(2,1)S(1)} %get-tuple-element.12.llo, bf16[512,1024]{1,0:T(8,128)(2,1)S(1)} %get-tuple-element.13.uhi, bf16[512,1024]{1,0:T(8,128)(2,1)S(1)} %get-tuple-element.14.ulo, ...), custom_call_target="tpu_custom_call" | custom-call | flops 1610612736 | bytes 8388608 | tf_op jit(solution)/shard_map/finish/pallas_call | solution.py:568
Async XLA Ops:
  0.0 54.3 %copy-start = (s32[8,8]{1,0:T(8,128)S(1)}, s32[8,8]{1,0:T(8,128)}, u32[]{:S(2)}) copy-start(s32[8,8]{1,0:T(8,128)} %pat_hbm.3) | copy-start | bytes 772

commit v4 on v3

--- a/solution.py
+++ b/solution.py
@@ -28,7 +28,16 @@
 def bit(mask, n):
     low, high = mask & 0xFFFF, mask >> 16
     half = jnp.where(n >= 16, jnp.int32(high), jnp.int32(low))
-    return lax.rem(lax.shift_right_logical(half, lax.rem(n, 16)), 2)
+    rest = lax.shift_right_logical(half, jnp.where(n >= 16, n - 16, n))
+    return rest - 2 * lax.shift_right_logical(rest, 1)
+
+
+def wrap(place, count):
+    return jnp.where(place == count, 0, place)
+
+
+def around(place, count):
+    return wrap(place + 1, count), jnp.where(place == 0, count - 1, place - 1)
 
 
 def lag(depth):
@@ -64,13 +73,11 @@
     lrecv, crecv, hrecv, urecv, lsend, csend, hsend, usend, uhand, load_sems,
 ):
     p, q = lax.axis_index("prow"), lax.axis_index("pcol")
-    y, core = lax.div(p, 2), lax.rem(p, 2)
-    z, x = lax.div(q, NX), lax.rem(q, NX)
+    y, z = lax.shift_right_logical(p, 1), lax.shift_right_logical(q, 2)
+    core, x = p - 2 * y, q - NX * z
     is_root = (q == 0) | (p == 0)
 
-    xp, xm = lax.rem(x + 1, NX), lax.rem(x + NX - 1, NX)
-    zp, zm = lax.rem(z + 1, NZ), lax.rem(z + NZ - 1, NZ)
-    yp, ym = lax.rem(y + 1, NY), lax.rem(y + NY - 1, NY)
+    (xp, xm), (yp, ym), (zp, zm) = around(x, NX), around(y, NY), around(z, NZ)
     ways = (z * NX + xp, z * NX + xm, zp * NX + x, zm * NX + x)
     rows = (yp * 2 + core, ym * 2 + core)
     mate = y * 2 + 1 - core
@@ -111,6 +118,10 @@
             ref = lbuf.at[part(tick, count), t, 1]
         return copy_l(ref, lsend.at[way], lrecv.at[4 * tick + t], y * 2 + 1, ways[way])
 
+    def send_leaf(even, tick, t, way):
+        ref = lbuf.at[tick, t, 0]
+        return copy_l(ref, lsend.at[way], hrecv.at[4 * even + t], y * 2, ways[way])
+
     def root_l(stream, tick, t, count=None):
         ref = lbuf.at[part(tick, count), t, stream]
         way = ROOT_WAY[t]
@@ -178,11 +189,17 @@
             lhi[into, column * B : (column + 1) * B] = hi
             llo[into, column * B : (column + 1) * B] = lo
 
+    childless = [(1 << 32) - 1 - functools.reduce(lambda m, n: m | n, CHILD[c]) for c in (0, 1)]
+
     used, tree_of, depth_of = [jnp.int32(0)] * 4, [jnp.int32(0)] * 4, [jnp.int32(0)] * 4
-    first_of, leaf = [jnp.int32(0)] * 4, [jnp.int32(1)] * 4
+    first_of, leaf, to_leaf = [jnp.int32(0)] * 4, [jnp.int32(1)] * 4, [jnp.int32(0)] * 4
+    mirrored = [
+        wrap(NZ - zz, NZ) * NX + wrap(NX - xx, NX)
+        for zz, xx in ((z, xp), (z, xm), (zp, x), (zm, x))
+    ]
     depths = []
     for t in range(4):
-        n = q if t < 2 else lax.rem(NZ - z, NZ) * NX + lax.rem(NX - x, NX)
+        n = q if t < 2 else wrap(NZ - z, NZ) * NX + wrap(NX - x, NX)
         tree, flip = t % 2, 0 if t < 2 else 1
         depths.append(sum(bit(DEPTH[tree][b], n) * (1 << b) for b in range(3)))
         for w in range(4):
@@ -192,44 +209,61 @@
             used[w] = used[w] + has
             tree_of[w] = tree_of[w] + has * t
             depth_of[w] = depth_of[w] + has * depths[t]
+            to = ways[w] if t < 2 else mirrored[w]
+            to_leaf[w] = to_leaf[w] + has * bit(childless[tree], to)
     deepest = jnp.maximum(functools.reduce(jnp.maximum, depths), 5)
 
-    def ready(pair, stream):
-        if stream == 0:
-
-            def wait_tick(i):
-                for t in range(4):
-                    hand_l(pair * 4 * R + 2 * i, t).wait_recv()
-
-            loop(2 * R, wait_tick)
-        else:
+    def right(pair, stream):
+        if stream == 1:
             loop(16, lambda i: wait_u(pair * 16 + i))
 
-        def split_both(i):
+        def split_right(i):
             for h in (0, 1):
                 for half in (0, 1):
-                    split_block(stream, 4 * pair + 2 * h + half, i, 4 * half + i, h)
                     j = 4 * half + i
                     hi, lo = split(get_u((2 * pair + h) * 8 + j))
                     uhi[h * B : (h + 1) * B, at(j)] = hi
                     ulo[h * B : (h + 1) * B, at(j)] = lo
 
-        loop(4, split_both)
-
-    def piece(n, stream):
+        loop(4, split_right)
+
+    def split_left(pair, half, stream):
+        def body(i):
+            for h in (0, 1):
+                split_block(stream, 4 * pair + 2 * h + half, i, 4 * half + i, h)
+
+        loop(4, body)
+
+    def piece(n, halves, stream):
         pair = lax.shift_right_logical(n, 2)
         tile = n - 4 * pair
-        pl.when(tile == 0)(lambda: ready(pair, stream))
+
+        @pl.when(tile == 0)
+        def _():
+            if 0 in halves:
+                pl.when(pair < 3)(lambda: right(pair, stream))
+            if stream == 0:
+
+                def wait_tick(i):
+                    for t in range(4):
+                        hand_l(pair * 4 * R + 2 * i, t).wait_recv()
+
+                loop(2 * R, wait_tick)
+            for half in halves:
+                split_left(pair, half, stream)
 
         @pl.when(pair < 3)
         def _():
-            cols = at(tile, 256)
-            a[:, cols] -= dot3(
-                (lhi[:, 0:256], llo[:, 0:256]), (uhi[0:256, cols], ulo[0:256, cols])
+            r, cols = slice(halves[0] * 512, (halves[-1] + 1) * 512), at(tile, 256)
+            a[r, cols] -= dot3(
+                (lhi[r, 0:256], llo[r, 0:256]), (uhi[0:256, cols], ulo[0:256, cols])
             )
 
+        if 1 in halves:
+            pl.when((pair == 2) & (tile == 3))(lambda: right(3, stream))
+
     def general0():
-        start = 4 * deepest + 6
+        first = 2 * deepest + 2
 
         def relay(tick, way):
             row = lax.shift_right_logical(tick, 2)
@@ -245,26 +279,27 @@
                 for way in (0, 1):
                     tick = 2 * kk + odd - LAG_U * (y if way == 0 else NY - y)
                     pl.when((tick >= 0) & (tick < 32))(lambda: relay(tick, way))
-            n = 2 * kk - start
-            pl.when(n >= 0)(lambda: piece(lax.shift_right_logical(n, 1), 0))
-
-        loop(lax.shift_right_logical(start, 1) + 13, step)
+            pl.when(kk >= first)(lambda: piece(kk - first, (0, 1), 0))
+
+        loop(first + 13, step)
         pl.when(y < NY - 1)(lambda: end_u(usend.at[0], 32))
         pl.when(y > 1)(lambda: end_u(usend.at[1], 32))
         end_u(uhand, 64)
 
     def general1(both):
         start = lag(deepest) + 4 * R + (0 if both else 4 * R)
+        first_piece = lax.shift_right_logical(start, 1)
         ticks = TICKS_L + (0 if both else 4 * R)
 
-        def receive(i, t, odd):
+        def receive(i, t, odd, is_leaf):
             def hand():
                 if odd:
                     hand_l(i - 1, t).start()
 
             if both:
-                send_l(i, t, 0, True).wait_recv()
-                hand()
+                send_l(i, t, 0, not is_leaf).wait_recv()
+                if not is_leaf:
+                    hand()
                 return
 
             @pl.when(i < 4 * R)
@@ -274,10 +309,16 @@
 
             pl.when(i >= 4 * R)(lambda: send_l(i - 4 * R, t, 0, False).wait_recv())
 
-        def forward(i, way):
+        def forward(i, way, odd):
             t = tree_of[way]
             if both:
-                send_l(i, t, way, True).start()
+                pl.when(to_leaf[way] == 0)(lambda: send_l(i, t, way, True).start())
+
+                @pl.when(to_leaf[way] == 1)
+                def _():
+                    send_leaf(i - 1 if odd else i, i, t, way).start()
+                    send_l(i, t, way, False).start()
+
                 return
             pl.when(i < 4 * R)(lambda: send_c(i, t, way).start())
             pl.when(i >= 4 * R)(lambda: send_l(i - 4 * R, t, way, False).start())
@@ -293,24 +334,19 @@
 
                 @pl.when((i >= 0) & (i < last[way]))
                 def _():
-                    pl.when(first_of[way] == 1)(lambda: receive(i, tree_of[way], odd))
-                    forward(i, way)
+                    pl.when(first_of[way] == 1)(lambda: receive(i, tree_of[way], odd, False))
+                    forward(i, way, odd)
 
             for t in range(4):
                 i = k - lags[t]
-                pl.when((i >= 0) & (i < last_leaf[t]))(lambda: receive(i, t, odd))
+                pl.when((i >= 0) & (i < last_leaf[t]))(lambda: receive(i, t, odd, True))
 
         def step(kk):
-            relay(2 * kk, False)
-            relay(2 * kk + 1, True)
-            n = 2 * kk - start
-            if R == 2:
-                pl.when(n >= 0)(lambda: piece(lax.shift_right_logical(n, 1), 1))
-            else:
-                even = (n & 2) == 0
-                pl.when((n >= 0) & even)(lambda: piece(lax.shift_right_logical(n, 2), 1))
-
-        loop(lax.shift_right_logical(start + 12 * R, 1) + 1, step)
+            for odd in (0, 1):
+                relay(2 * kk + odd, odd == 1)
+                pl.when(kk >= first_piece)(lambda: piece(kk - first_piece, (odd,), 1))
+
+        loop(first_piece + 13, step)
         for way in range(4):
 
             @pl.when(used[way] == 1)
@@ -319,7 +355,14 @@
                 if not both:
                     send_c(0, 0, way, 4 * R).wait_send()
 
-        hand_ticks(0, TICKS_L if both else 4 * R).wait_send()
+        if both:
+            handed = 4 - sum(leaf)
+            for count in range(1, 5):
+                pl.when(handed == count)(
+                    lambda: copy_l(lbuf.at[:, pl.ds(0, count), 0], hsend, hrecv.at[0], mate, q).wait_send()
+                )
+        else:
+            hand_ticks(0, 4 * R).wait_send()
 
     def mask_block(i, j):
         block = a[at(i), at(j)] * keep(i, j)

time: 58.4 us -> 58.2 us (level)
  no operation moved by 1% of the time
where the time goes in v4:
time: 58.2 us; the launch traced here: 58.1 us
  Pallas kernels  57.9 us (99%)
    pallas_call x1, Pallas kernels, shards(): pl.pallas_call(kernel, out_shape=[pltpu.VMEM(matrix.shape, f32)] + [pltpu...  54.1 us
    pallas_call x1, Pallas kernels, shards(): pl.pallas_call(finish, out_shape=jax.ShapeDtypeStruct(matrix.shape, f32),...  3.81 us

profile of v4, /device:TPU:40, one launch (start us, length us, event | category | flops | bytes accessed | tf_op | source)
XLA Modules:
  0.0 58.1 jit_solution(1802629131506108042)
XLA Ops:
  0.0 0.0 copy-start
  0.0 54.1 %factor.1 = (f32[1024,1024]{1,0:T(8,128)S(1)}, bf16[1024,512]{1,0:T(8,128)(2,1)S(1)}, bf16[1024,512]{1,0:T(8,128)(2,1)S(1)}, bf16[512,1024]{1,0:T(8,128)(2,1)S(1)}, bf16[512,1024]{1,0:T(8,128)(2,1)S(1)}) custom-call(f32[1024,1024]{1,0:T(8,128)} %a_hbm.1, f32[8,128,128]{2,1,0:T(8,128)} %pinv_hbm.1, s32[8,8]{1,0:T(8,128)} %pat_hbm.3), custom_call_target="tpu_custom_call" | custom-call | flops 5368709120 | bytes 8388608 | tf_op jit(solution)/shard_map/factor/pallas_call | solution.py:580
  54.1 0.0 copy-done
  54.1 3.8 %finish.1 = f32[1024,1024]{1,0:T(8,128)} custom-call(f32[1024,1024]{1,0:T(8,128)S(1)} %get-tuple-element.10.a, bf16[1024,512]{1,0:T(8,128)(2,1)S(1)} %get-tuple-element.11.lhi, bf16[1024,512]{1,0:T(8,128)(2,1)S(1)} %get-tuple-element.12.llo, bf16[512,1024]{1,0:T(8,128)(2,1)S(1)} %get-tuple-element.13.uhi, bf16[512,1024]{1,0:T(8,128)(2,1)S(1)} %get-tuple-element.14.ulo, ...), custom_call_target="tpu_custom_call" | custom-call | flops 1610612736 | bytes 8388608 | tf_op jit(solution)/shard_map/finish/pallas_call | solution.py:611
Async XLA Ops:
  0.0 54.1 %copy-start = (s32[8,8]{1,0:T(8,128)S(1)}, s32[8,8]{1,0:T(8,128)}, u32[]{:S(2)}) copy-start(s32[8,8]{1,0:T(8,128)} %pat_hbm.3) | copy-start | bytes 772

commit v5 on v4

--- a/solution.py
+++ b/solution.py
@@ -549,19 +549,18 @@
         load = pltpu.make_async_copy(pat_hbm, pat, pat_sem)
         load.start()
         copies = []
-        for tile in range(4):
-            cols = slice(tile * 256, (tile + 1) * 256)
+        for n, (first, last) in enumerate(((0, 512), (512, 768), (768, 1024))):
+            cols = slice(first, last)
             right = (uhi[0:256, cols], ulo[0:256, cols])
-            tiles[tile] = a[:, cols] - dot3((lhi[:, 0:256], llo[:, 0:256]), right)
-            if tile == 0:
+            tiles[:, cols] = a[:, cols] - dot3((lhi[:, 0:256], llo[:, 0:256]), right)
+            if n == 0:
                 load.wait()
             for i in range(8):
-                for h in (0, 1):
-                    r, c = slice(i * B, (i + 1) * B), slice(h * B, (h + 1) * B)
-                    keep = pat[i, 2 * tile + h].astype(jnp.float32)
-                    tiles[tile, r, c] = tiles[tile, r, c] * keep
+                for j in range(first // B, last // B):
+                    r, c = slice(i * B, (i + 1) * B), slice(j * B, (j + 1) * B)
+                    tiles[r, c] = tiles[r, c] * pat[i, j].astype(jnp.float32)
             copies.append(
-                pltpu.make_async_copy(tiles.at[tile], out.at[:, cols], out_sems.at[tile])
+                pltpu.make_async_copy(tiles.at[:, cols], out.at[:, cols], out_sems.at[n])
             )
             copies[-1].start()
         for copy in copies:
@@ -614,7 +613,7 @@
         in_specs=[in_vmem] * 5 + [in_hbm],
         out_specs=in_hbm,
         scratch_shapes=[
-            pltpu.VMEM((4, 1024, 256), f32),
+            pltpu.VMEM((1024, 1024), f32),
             pltpu.SMEM(pattern.shape, jnp.int32),
             pltpu.SemaphoreType.DMA,
             pltpu.SemaphoreType.DMA((4,)),

time: 58.2 us -> 58.2 us (level)
  no operation moved by 1% of the time
where the time goes in v5:
time: 58.2 us
  Pallas kernels  58 us (100%)
    pallas_call x1, Pallas kernels, shards(): pl.pallas_call(kernel, out_shape=[pltpu.VMEM(matrix.shape, f32)] + [pltpu...  54.1 us
    pallas_call x1, Pallas kernels, shards(): pl.pallas_call(finish, out_shape=jax.ShapeDtypeStruct(matrix.shape, f32),...  3.89 us

profile of v5, /device:TPU:40, one launch (start us, length us, event | category | flops | bytes accessed | tf_op | source)
XLA Modules:
  0.0 58.2 jit_solution(13087142727840180705)
XLA Ops:
  0.0 0.0 copy-start
  0.0 54.1 %factor.1 = (f32[1024,1024]{1,0:T(8,128)S(1)}, bf16[1024,512]{1,0:T(8,128)(2,1)S(1)}, bf16[1024,512]{1,0:T(8,128)(2,1)S(1)}, bf16[512,1024]{1,0:T(8,128)(2,1)S(1)}, bf16[512,1024]{1,0:T(8,128)(2,1)S(1)}) custom-call(f32[1024,1024]{1,0:T(8,128)} %a_hbm.1, f32[8,128,128]{2,1,0:T(8,128)} %pinv_hbm.1, s32[8,8]{1,0:T(8,128)} %pat_hbm.3), custom_call_target="tpu_custom_call" | custom-call | flops 5368709120 | bytes 8388608 | tf_op jit(solution)/shard_map/factor/pallas_call | solution.py:579
  54.1 0.0 copy-done
  54.1 3.9 %finish.1 = f32[1024,1024]{1,0:T(8,128)} custom-call(f32[1024,1024]{1,0:T(8,128)S(1)} %get-tuple-element.10.a, bf16[1024,512]{1,0:T(8,128)(2,1)S(1)} %get-tuple-element.11.lhi, bf16[1024,512]{1,0:T(8,128)(2,1)S(1)} %get-tuple-element.12.llo, bf16[512,1024]{1,0:T(8,128)(2,1)S(1)} %get-tuple-element.13.uhi, bf16[512,1024]{1,0:T(8,128)(2,1)S(1)} %get-tuple-element.14.ulo, ...), custom_call_target="tpu_custom_call" | custom-call | flops 1610612736 | bytes 8388608 | tf_op jit(solution)/shard_map/finish/pallas_call | solution.py:610
Async XLA Ops:
  0.0 54.1 %copy-start = (s32[8,8]{1,0:T(8,128)S(1)}, s32[8,8]{1,0:T(8,128)}, u32[]{:S(2)}) copy-start(s32[8,8]{1,0:T(8,128)} %pat_hbm.3) | copy-start | bytes 772
